TPU v7x, 32 devices: a whole 2x2x4 slice. The times are simulated.
32 devices in a mesh: parts: 1, row: 8 (over z, y), col: 1, depth: 4 (over x, core).
Axes of the slice: x: 2, y: 2, z: 4, core: 2. Of those that a mesh axis runs over, the one named last changes fastest.
Arguments:
- activations: bfloat16 [4, 256, 8192], P(('parts', 'depth'), 'row', 'col'), may hold values from -6 to 6
- hidden_grads: bfloat16 [4, 256, 16384], P(('parts', 'depth'), 'col', 'row'), may hold values from -0.1875 to 0.1875
Outputs:
- weight_grad: bfloat16 [8192, 16384], P(('parts', 'col', 'depth'), 'row')
All inputs are finite; a program needn't handle non-finite values.
Results may differ from a plain program's by a relative error of at most 0.013.
Values may be sent and summed in bfloat16 or wider, within the bound.
A program may use at most 128 MiB of HBM per device.

v0:
```python
import jax
import jax.numpy as jnp
from jax import lax
from jax.sharding import PartitionSpec as P


def local(activations, hidden_grads):
    swapped = lax.all_to_all(activations, "depth", split_axis=2, concat_axis=0, tiled=True)
    acts = lax.all_gather(swapped, "row", axis=1, tiled=True)
    grads = lax.all_gather(hidden_grads, "depth", axis=0, tiled=True)
    grads = lax.all_gather(grads, "col", axis=1, tiled=True)
    total = lax.dot_general(
        acts, grads, (((0, 1), (0, 1)), ((), ())), preferred_element_type=jnp.float32
    )
    return total.astype(jnp.bfloat16)


def solution(mesh):
    in_specs = (P(("parts", "depth"), "row", "col"), P(("parts", "depth"), "col", "row"))
    out_specs = P(("parts", "col", "depth"), "row")
    return jax.shard_map(local, mesh=mesh, in_specs=in_specs, out_specs=out_specs, check_vma=False)
```

profile of v0, /device:TPU:0, one launch (start us, length us, event | category | flops | bytes accessed | tf_op | source)
XLA Modules:
  0.0 217.2 jit_solution(3695399159835913625)
XLA Ops:
  6.5 0.0 all-gather.6.cloned.1.call-start
  6.5 8.6 %copy.7 = bf16[1,32,8192]{1,0,2:T(2,128)(2,1)} copy(bf16[1,32,8192]{2,1,0:T(8,128)(2,1)} %param.2) | data formatting | bytes 1048576 | tf_op args[0]
  15.1 0.5 broadcast
  15.6 45.2 %reduce = bf16[8192,32]{1,0:T(8,128)(2,1)S(1)} reduce(bf16[8192,1,32]{2,1,0:T(2,128)(2,1)} %bitcast.11, bf16[]{:T(256)} %broadcast), dimensions={1}, to_apply=%bitcast.8.reduce_sub_computation | reduce | bytes 1048578
  60.8 2.2 reshape.2
  63.0 12.9 %all_to_all.18 = bf16[4,2,32768]{2,1,0:T(2,128)(2,1)S(1)} all-to-all(bf16[4,2,32768]{2,1,0:T(2,128)(2,1)S(1)} %reshape.2), channel_id=1, replica_groups=mesh['parts'=1,'row'=8,'col'=1,'depth'=4] {'depth'}, dimensions={0} | all-to-all | bytes 1048576 | tf_op jit(solution)/shard_map/all_to_all | solution.py:8
  75.9 3.3 %reshape.3 = bf16[8192,1,32]{2,1,0:T(2,128)(2,1)} reshape(bf16[4,2,32768]{2,1,0:T(2,128)(2,1)S(1)} %all_to_all.18) | data formatting | bytes 1048576
  79.1 8.0 %copy.8 = bf16[1,32,8192]{2,1,0:T(8,128)(2,1)S(1)} copy(bf16[1,32,8192]{1,0,2:T(2,128)(2,1)} %bitcast.12) | data formatting | bytes 1048576 | tf_op jit(solution)/shard_map/all_to_all | solution.py:8
  87.1 1.2 all_to_all.14
  88.3 0.0 all-gather.6.cloned.1.call-update
  88.3 0.2 all-gather.4.cloned.1.call-start
  88.5 0.5 all-gather.4.cloned.1.call-update
  89.0 73.1 %all-gather.6.cloned.1.call-done = bf16[4,1,256,2048]{3,0,1,2:T(4,128)(2,1)} async-done(((bf16[4,1,32,2048]{3,0,1,2:T(4,128)(2,1)}), bf16[4,1,256,2048]{3,0,1,2:T(4,128)(2,1)}) %all-gather.6.cloned.1.call-update) | async-done | bytes 4194320 | tf_op jit(solution)/shard_map/all_gather | solution.py:9
  162.2 7.6 %copy.10 = bf16[4,1,256,2048]{2,3,0,1:T(8,128)(2,1)} copy(bf16[4,1,256,2048]{3,0,1,2:T(4,128)(2,1)} %all-gather.6.cloned.1.call-done) | data formatting | bytes 8388608 | tf_op jit(solution)/shard_map/all_gather | solution.py:9
  169.7 26.8 %all-gather.4.cloned.1.call-done = bf16[4,256,2048]{2,1,0:T(8,128)(2,1)} async-done(((bf16[1,256,2048]{2,1,0:T(8,128)(2,1)}), bf16[4,256,2048]{2,1,0:T(8,128)(2,1)}) %all-gather.4.cloned.1.call-update) | async-done | bytes 4194320 | tf_op jit(solution)/shard_map/all_gather | solution.py:10
  196.5 13.9 %bitcast_convert_fusion = bf16[2048,2048]{1,0:T(8,128)(2,1)} fusion(bf16[4,256,2048]{2,1,0:T(8,128)(2,1)} %all-gather.4.cloned.1.call-done, bf16[4,1,256,2048]{2,3,0,1:T(8,128)(2,1)} %copy.10), kind=kOutput, calls=%fused_computation | convolution fusion | flops 8594128896 | bytes 16777216 | tf_op jit(solution)/shard_map/dot_general | solution.py:12
Async XLA Ops:
  6.5 155.6 %all-gather.6.cloned.1.call-start = ((), (), s32[]{:S(2)}) async-start(), calls=%async_computation.2 | async-start | bytes 4718592 | tf_op jit(solution)/shard_map/all_gather | solution.py:9
  88.3 108.2 %all-gather.4.cloned.1.call-start = ((), (), s32[]{:S(2)}) async-start(), calls=%async_computation.1 | async-start | bytes 5242880 | tf_op jit(solution)/shard_map/all_gather | solution.py:10
Sparse Core Ops, SparseCore 0:
  88.4 73.7 all-gather.5
  163.7 32.7 all-gather.3
where the time goes:
time: 218 us; the launch traced here: 217 us
  waiting for transfers between devices  100 us (46%)
  other arithmetic  45.2 us (21%)
  local copies, waits for them, and re-layouts  31.2 us (14%)
  matrix products  13.9 us (6%)
  between operations  13.4 us (6%)
  blocking collectives  12.9 us (6%)
    all_gather x1, waiting for transfers between devices, local(): acts = lax.all_gather(swapped, 'row', axis=1, tiled=True)  73.1 us
    unnamed x1, other arithmetic  45.2 us
    all_gather x1, waiting for transfers between devices, local(): grads = lax.all_gather(hidden_grads, 'depth', axis=0, tiled=True)  26.8 us
    unnamed x4, local copies, waits for them, and re-layouts  14.5 us
    dot_general x1, matrix products, local(): lax.dot_general(acts, grads, (((0, 1), (0, 1)), ((), ())), preferred_elem...  13.9 us
    all_to_all x1, blocking collectives, local(): lax.all_to_all(activations, 'depth', split_axis=2, concat_axis=0, tiled=T...  12.9 us
    all_to_all x2, local copies, waits for them, and re-layouts, local(): lax.all_to_all(activations, 'depth', split_axis=2, concat_axis=0, tiled=T...  9.14 us
    all_gather x1, local copies, waits for them, and re-layouts, local(): acts = lax.all_gather(swapped, 'row', axis=1, tiled=True)  7.56 us
  transfers between devices with their start and end apart: 2, of which 2 were waited for; matrix products, arithmetic and copies ran while one was open for 3% of the time, Pallas kernels for 0%

commit v1 on v0

--- a/solution.py
+++ b/solution.py
@@ -4,8 +4,27 @@
 from jax.sharding import PartitionSpec as P
 
 
+def in_blocks(x, dim, size):
+    before, after = (x.shape[:dim], x.shape[dim + 1 :])
+    return jnp.moveaxis(x.reshape(*before, size, -1, *after), dim, 0)
+
+
+def laid_out(tiles, dim):
+    tiles = jnp.moveaxis(tiles, 0, dim)
+    shape = tiles.shape
+    return tiles.reshape(*shape[:dim], shape[dim] * shape[dim + 1], *shape[dim + 2 :])
+
+
 def local(activations, hidden_grads):
-    swapped = lax.all_to_all(activations, "depth", split_axis=2, concat_axis=0, tiled=True)
+    size, place = (lax.axis_size("depth"), lax.axis_index("depth"))
+    pieces = in_blocks(activations, 2, size)
+    filled = pieces
+    for lap in range(1, size):
+        target, source = ((place + lap) % size, (place - lap) % size)
+        sent = lax.dynamic_index_in_dim(pieces, target, 0)
+        partner_block = lax.ppermute(sent, "depth", [(i, (i + lap) % size) for i in range(size)])
+        filled = lax.dynamic_update_slice_in_dim(filled, partner_block, source, axis=0)
+    swapped = laid_out(filled, 0)
     acts = lax.all_gather(swapped, "row", axis=1, tiled=True)
     grads = lax.all_gather(hidden_grads, "depth", axis=0, tiled=True)
     grads = lax.all_gather(grads, "col", axis=1, tiled=True)

time: 218 us -> 143 us (0.66)
  other arithmetic: 45.2 us -> 0 us
  local copies, waits for them, and re-layouts: 31.2 us -> 3.36 us
  blocking collectives: 12.9 us -> 0 us
  waiting for transfers between devices: 100 us -> 107 us
  starting transfers between devices: 0.22 us -> 4.61 us
    unnamed x1 -> x0, other arithmetic: 45.2 us -> none
    unnamed x4 -> x7, local copies, waits for them, and re-layouts: 14.5 us -> 1.04 us
    all_to_all x1 -> x0, blocking collectives: 12.9 us -> none  [local(): lax.all_to_all(activations, 'depth', split_axis=2, concat_axis=0, tiled=T...]
    all_to_all x2 -> x0, local copies, waits for them, and re-layouts: 9.14 us -> none  [local(): lax.all_to_all(activations, 'depth', split_axis=2, concat_axis=0, tiled=T...]
    all_gather x1 -> x0, local copies, waits for them, and re-layouts: 7.56 us -> none  [local(): acts = lax.all_gather(swapped, 'row', axis=1, tiled=True)]
    ppermute x0 -> x3, starting transfers between devices: none -> 4.57 us  [local(): lax.ppermute(sent, 'depth', [(i, (i + lap) % size) for i in range(size)])]
    ppermute x0 -> x3, waiting for transfers between devices: none -> 4.29 us  [local(): lax.ppermute(sent, 'depth', [(i, (i + lap) % size) for i in range(size)])]
    all_gather x1, waiting for transfers between devices: 73.1 us -> 75.6 us  [local(): acts = lax.all_gather(swapped, 'row', axis=1, tiled=True)]
  transfers between devices with their start and end apart: 2 -> 5, of which waited for: 2 -> 5; matrix products, arithmetic and copies ran while one was open for 3% -> 2% of each run, Pallas kernels for 0% -> 0%
where the time goes in v1:
time: 143 us
  waiting for transfers between devices  107 us (75%)
  matrix products  14 us (10%)
  between operations  13.5 us (9%)
  starting transfers between devices  4.61 us (3%)
  local copies, waits for them, and re-layouts  3.36 us (2%)
    all_gather x1, waiting for transfers between devices, local(): acts = lax.all_gather(swapped, 'row', axis=1, tiled=True)  75.6 us
    all_gather x1, waiting for transfers between devices, local(): grads = lax.all_gather(hidden_grads, 'depth', axis=0, tiled=True)  26.5 us
    dot_general x1, matrix products, local(): lax.dot_general(acts, grads, (((0, 1), (0, 1)), ((), ())), preferred_elem...  14 us
    ppermute x3, starting transfers between devices, local(): lax.ppermute(sent, 'depth', [(i, (i + lap) % size) for i in range(size)])  4.57 us
    ppermute x3, waiting for transfers between devices, local(): lax.ppermute(sent, 'depth', [(i, (i + lap) % size) for i in range(size)])  4.29 us
  transfers between devices with their start and end apart: 5, of which 5 were waited for; matrix products, arithmetic and copies ran while one was open for 2% of the time, Pallas kernels for 0%

profile of v1, /device:TPU:0, one launch (start us, length us, event | category | flops | bytes accessed | tf_op | source)
XLA Modules:
  0.0 142.6 jit_solution(15523267363646797287)
XLA Ops:
  6.5 0.0 copy-start
  6.5 0.0 all-gather.5.cloned.1.call-start
  6.5 0.7 all-gather.5.cloned.1.call-update
  7.3 0.0 all-gather.3.cloned.1.call-start
  7.3 1.4 %reshape.21 = bf16[1,32,4,2048]{3,2,1,0:T(4,128)(2,1)S(1)} reshape(bf16[1,32,8192]{2,1,0:T(8,128)(2,1)} %param.2) | data formatting | bytes 1048576 | tf_op jit(solution)/shard_map/reshape | solution.py:9
  8.8 0.8 constant_dynamic-slice_fusion
  9.6 0.1 copy.17
  9.7 0.5 collective-permute-start
  10.2 0.1 copy.16
  10.3 2.6 %collective-permute-start.1 = (bf16[1,1,32,2048]{3,2,1,0:T(8,128)(2,1)S(1)}, bf16[1,1,32,2048]{3,2,1,0:T(8,128)(2,1)S(1)}, u32[]{:S(2)}, u32[]{:S(2)}) collective-permute-start(bf16[1,1,32,2048]{3,2,1,0:T(8,128)(2,1)S(1)} %bitcast.31), channel_id=1, source_target_pairs={{0,2},{1,3},{2,0},{3,1},{4,6},{5,7},{6,4},{7,5},{8,10},{9,11},{10,... | collective-permute-start | bytes 393224 | tf_op jit(solution)/shard_map/ppermute | solution.py:25
  12.9 0.1 copy.15
  12.9 1.5 %collective-permute-start.2 = (bf16[1,1,32,2048]{3,2,1,0:T(8,128)(2,1)S(1)}, bf16[1,1,32,2048]{3,2,1,0:T(8,128)(2,1)S(1)}, u32[]{:S(2)}, u32[]{:S(2)}) collective-permute-start(bf16[1,1,32,2048]{3,2,1,0:T(8,128)(2,1)S(1)} %bitcast.30), channel_id=1, source_target_pairs={{0,3},{1,0},{2,1},{3,2},{4,7},{5,4},{6,5},{7,6},{8,11},{9,8},{10,9... | collective-permute-start | bytes 393224 | tf_op jit(solution)/shard_map/ppermute | solution.py:25
  14.4 0.0 copy-done
  14.5 0.7 collective-permute-done
  15.2 1.6 %collective-permute-done.1 = bf16[1,1,32,2048]{3,2,1,0:T(8,128)(2,1)S(1)} collective-permute-done((bf16[1,1,32,2048]{3,2,1,0:T(8,128)(2,1)S(1)}, bf16[1,1,32,2048]{3,2,1,0:T(8,128)(2,1)S(1)}, u32[]{:S(2)}, u32[]{:S(2)}) %collective-permute-start.1) | collective-permute-done | bytes 131104 | tf_op jit(solution)/shard_map/ppermute | solution.py:25
  16.8 2.0 %collective-permute-done.2 = bf16[1,1,32,2048]{3,2,1,0:T(8,128)(2,1)S(1)} collective-permute-done((bf16[1,1,32,2048]{3,2,1,0:T(8,128)(2,1)S(1)}, bf16[1,1,32,2048]{3,2,1,0:T(8,128)(2,1)S(1)}, u32[]{:S(2)}, u32[]{:S(2)}) %collective-permute-start.2) | collective-permute-done | bytes 131104 | tf_op jit(solution)/shard_map/ppermute | solution.py:25
  18.8 0.0 copy-start.1
  18.9 0.8 copy-done.1
  19.6 0.0 all-gather.3.cloned.1.call-update
  19.7 26.5 %all-gather.5.cloned.1.call-done = bf16[4,256,2048]{2,1,0:T(8,128)(2,1)} async-done(((bf16[1,256,2048]{2,1,0:T(8,128)(2,1)}), bf16[4,256,2048]{2,1,0:T(8,128)(2,1)}) %all-gather.5.cloned.1.call-update) | async-done | bytes 4194320 | tf_op jit(solution)/shard_map/all_gather | solution.py:29
  46.1 75.6 %all-gather.3.cloned.1.call-done = bf16[4,256,2048]{2,1,0:T(8,128)(2,1)} async-done(((bf16[4,32,2048]{2,1,0:T(8,128)(2,1)}), bf16[4,256,2048]{2,1,0:T(8,128)(2,1)}) %all-gather.3.cloned.1.call-update) | async-done | bytes 4194320 | tf_op jit(solution)/shard_map/all_gather | solution.py:28
  121.7 14.0 %bitcast_convert_fusion = bf16[2048,2048]{1,0:T(8,128)(2,1)} fusion(bf16[4,256,2048]{2,1,0:T(8,128)(2,1)} %all-gather.3.cloned.1.call-done, bf16[4,256,2048]{2,1,0:T(8,128)(2,1)} %all-gather.5.cloned.1.call-done), kind=kOutput, calls=%fused_computation | convolution fusion | flops 8594128896 | bytes 16777216 | tf_op jit(solution)/shard_map/dot_general | solution.py:31
  (4 shorter events, 0.1 us)
Async XLA Ops:
  6.5 7.9 %copy-start = (bf16[1,32,8192]{2,1,0:T(8,128)(2,1)S(1)}, bf16[1,32,8192]{2,1,0:T(8,128)(2,1)}, u32[]{:S(2)}) copy-start(bf16[1,32,8192]{2,1,0:T(8,128)(2,1)} %param.2) | copy-start | bytes 1572868
  6.5 39.6 %all-gather.5.cloned.1.call-start = ((), (), s32[]{:S(2)}) async-start(), calls=%async_computation.1 | async-start | bytes 5242880 | tf_op jit(solution)/shard_map/all_gather | solution.py:29
  7.3 114.5 %all-gather.3.cloned.1.call-start = ((), (), s32[]{:S(2)}) async-start(), calls=%async_computation | async-start | bytes 4718592 | tf_op jit(solution)/shard_map/all_gather | solution.py:28
  9.7 5.5 %collective-permute-start = (bf16[1,1,32,2048]{3,2,1,0:T(8,128)(2,1)S(1)}, bf16[1,1,32,2048]{3,2,1,0:T(8,128)(2,1)S(1)}, u32[]{:S(2)}, u32[]{:S(2)}) collective-permute-start(bf16[1,1,32,2048]{3,2,1,0:T(8,128)(2,1)S(1)} %bitcast.32), channel_id=1, source_target_pairs={{0,1},{1,2},{2,3},{3,0},{4,5},{5,6},{6,7},{7,4},{8,9},{9,10},{10,1... | collective-permute-start | bytes 393224 | tf_op jit(solution)/shard_map/ppermute | solution.py:25
  10.3 6.5 %collective-permute-start.1 = (bf16[1,1,32,2048]{3,2,1,0:T(8,128)(2,1)S(1)}, bf16[1,1,32,2048]{3,2,1,0:T(8,128)(2,1)S(1)}, u32[]{:S(2)}, u32[]{:S(2)}) collective-permute-start(bf16[1,1,32,2048]{3,2,1,0:T(8,128)(2,1)S(1)} %bitcast.31), channel_id=1, source_target_pairs={{0,2},{1,3},{2,0},{3,1},{4,6},{5,7},{6,4},{7,5},{8,10},{9,11},{10,... | collective-permute-start | bytes 393224 | tf_op jit(solution)/shard_map/ppermute | solution.py:25
  12.9 5.9 %collective-permute-start.2 = (bf16[1,1,32,2048]{3,2,1,0:T(8,128)(2,1)S(1)}, bf16[1,1,32,2048]{3,2,1,0:T(8,128)(2,1)S(1)}, u32[]{:S(2)}, u32[]{:S(2)}) collective-permute-start(bf16[1,1,32,2048]{3,2,1,0:T(8,128)(2,1)S(1)} %bitcast.30), channel_id=1, source_target_pairs={{0,3},{1,0},{2,1},{3,2},{4,7},{5,4},{6,5},{7,6},{8,11},{9,8},{10,9... | collective-permute-start | bytes 393224 | tf_op jit(solution)/shard_map/ppermute | solution.py:25
  18.8 0.8 copy-start.1
Sparse Core Ops, SparseCore 0:
  8.9 37.1 all-gather.4
  48.3 73.3 all-gather.2
